TPU v7x, 512 devices: a whole 4x4x16 slice. The times are simulated.
512 devices in a mesh: rep: 16 (over z_hi, y), fsdp: 32 (over z_lo, x, core).
Axes of the slice: x: 4, y: 4, z: 16 (z_hi: 4, z_lo: 4; z = z_hi * 4 + z_lo), core: 2. Of those that a mesh axis runs over, the one named last changes fastest.
Arguments:
- grad_parts: bfloat16 [16, 32, 128, 8192], P('rep', 'fsdp'), may hold values from -6 to 6
- momentum: float32 [16, 128, 8192], P('rep', None, 'fsdp'), may hold values from -6 to 6
Outputs:
- momentum_out: float32 [16, 128, 8192], P('rep', None, 'fsdp')
- update: float32 [128, 8192], P(None, 'fsdp')
All inputs are finite; a program needn't handle non-finite values.
Results may differ from a plain program's by a relative error of at most 0.0003.
Values sent between devices are 32-bit elements; how exact they have to be, the bound alone decides.
A program may use at most 64 MiB of HBM per device.

v0:
```python
import jax
import jax.numpy as jnp
from jax import lax
from jax.sharding import PartitionSpec as P

GROUP = 64
BAND = 8


def block_table(count):
    rows_idx = lax.broadcasted_iota(jnp.int32, (count * BAND, count * GROUP), 0)
    cols_idx = lax.broadcasted_iota(jnp.int32, (count * BAND, count * GROUP), 1)
    freq = (rows_idx % BAND).astype(jnp.float32)
    place = (cols_idx % GROUP).astype(jnp.float32)
    scale = jnp.where(freq == 0.0, jnp.sqrt(1.0 / GROUP), jnp.sqrt(2.0 / GROUP)).astype(jnp.float32)
    value = scale * jnp.cos(jnp.pi * (2.0 * place + 1.0) * freq / (2.0 * GROUP))
    same = rows_idx // BAND == cols_idx // GROUP
    return jnp.where(same, value, 0.0)


def body(grad_parts, momentum):
    local = grad_parts[0, 0].astype(jnp.float32)
    high = lax.Precision.HIGHEST
    col_table = block_table(momentum.shape[2] // GROUP)

    def inverse(coeffs, row_table):
        left = jnp.dot(row_table.T, coeffs, precision=high, preferred_element_type=jnp.float32)
        return jnp.dot(left, col_table, precision=high, preferred_element_type=jnp.float32)

    row_table = block_table(momentum.shape[1] // GROUP)
    grad = lax.psum_scatter(local, "fsdp", scatter_dimension=1, tiled=True)
    moment = 0.999 * momentum[0] + grad
    left = jnp.dot(row_table, moment, precision=high, preferred_element_type=jnp.float32)
    band = jnp.dot(left, col_table.T, precision=high, preferred_element_type=jnp.float32)
    momentum_out = moment - inverse(band, row_table)
    replicas = lax.axis_size("rep")
    every = lax.all_gather(band[None], "rep", axis=0, tiled=True)
    shared = jnp.sum(every, axis=0) / replicas
    update = inverse(shared, row_table)
    return (momentum_out[None], update)


def solution(mesh):
    in_specs = (P("rep", "fsdp", None, None), P("rep", None, "fsdp"))
    out_specs = (P("rep", None, "fsdp"), P(None, "fsdp"))
    return jax.shard_map(body, mesh=mesh, in_specs=in_specs, out_specs=out_specs, check_vma=False)
```

profile of v0, /device:TPU:128, one launch (start us, length us, event | category | flops | bytes accessed | tf_op | source)
XLA Modules:
  0.0 231.2 jit_solution(8169221663725408832)
XLA Ops:
  7.2 0.0 copy-start
  7.2 0.0 reduce-scatter.2.cloned.1.call-start
  7.2 4.0 %bitcast_convert_fusion = f32[128,8192]{1,0:T(8,128)} fusion(bf16[1,1,128,8192]{3,2,1,0:T(8,128)(2,1)} %param.2), kind=kLoop, calls=%fused_computation | loop fusion | flops 1048576 | bytes 6291456 | tf_op jit(solution)/shard_map/convert_element_type | solution.py:22
  11.2 0.0 reduce-scatter.2.cloned.1.call-update
  11.4 159.1 %reduce-scatter.2.cloned.1.call-done = f32[128,256]{1,0:T(8,128)} async-done(((f32[128,8192]{1,0:T(8,128)}), f32[128,256]{1,0:T(8,128)}) %reduce-scatter.2.cloned.1.call-update) | async-done | bytes 131088 | tf_op jit(solution)/shard_map/reduce_scatter | solution.py:31
  170.5 0.0 copy-done
  170.5 1.2 fusion.1
  171.7 0.3 fusion.5
  172.0 0.4 fusion.32
  172.5 48.3 %all-gather = f32[256,32]{1,0:T(8,128)S(1)} all-gather(f32[16,32]{1,0:T(8,128)S(1)} %fusion.5), channel_id=2, replica_groups=mesh['rep'=16,'fsdp'=32] {'rep'}, dimensions={0}, use_global_device_ids=true | all-gather | bytes 34816 | tf_op jit(solution)/shard_map/all_gather | solution.py:37
  220.8 0.4 fusion.2
  221.2 1.1 fusion.4
  222.3 2.0 fusion
  (13 shorter events, 0.1 us)
Async XLA Ops:
  7.2 163.3 %copy-start = (f32[1,128,256]{2,1,0:T(8,128)S(1)}, f32[1,128,256]{2,1,0:T(8,128)}, u32[]{:S(2)}) copy-start(f32[1,128,256]{2,1,0:T(8,128)} %param.3) | copy-start | bytes 393220
  7.2 163.3 %reduce-scatter.2.cloned.1.call-start = ((), (), s32[]{:S(2)}) async-start(), calls=%async_computation.1 | async-start | bytes 4325376 | tf_op jit(solution)/shard_map/reduce_scatter | solution.py:31
Sparse Core Ops, SparseCore 0:
  11.4 159.1 reduce-scatter.1
where the time goes:
time: 231 us
  waiting for transfers between devices  159 us (69%)
  blocking collectives  48.3 us (21%)
  between operations  14.1 us (6%)
  matrix products  5.47 us (2%)
  other arithmetic  4.08 us (2%)
    reduce_scatter x1, waiting for transfers between devices, body(): grad = lax.psum_scatter(local, 'fsdp', scatter_dimension=1, tiled=True)  159 us
    all_gather x1, blocking collectives, body(): every = lax.all_gather(band[None], 'rep', axis=0, tiled=True)  48.3 us
  transfers between devices with their start and end apart: 1, of which 1 were waited for; matrix products, arithmetic and copies ran while one was open for 0% of the time, Pallas kernels for 0%

commit v1 on v0

v1 whole, which is shorter than its diff:
```python
import jax
import jax.numpy as jnp
import numpy as np
from jax import lax
from jax.experimental import pallas as pl
from jax.experimental.pallas import tpu as pltpu
from jax.sharding import PartitionSpec as P

MESH = pl.DeviceIdType.MESH
F32, BF16 = jnp.float32, jnp.bfloat16
GROUP, BAND = 64, 8
ROWS, WIDTH = 128, 256
NX = NY = NL = NH = 4

PIECES = ((0, 32), (32, 32), (64, 32), (96, 32))
K = len(PIECES)
FAR, NEXT, PREV, OWN = 0, 1, 2, 3
STEP_OF_SLOT = (2, 1, 3, 0)


def tables():
    freq = np.arange(BAND)[:, None]
    place = np.arange(GROUP)[None, :]
    scale = np.where(freq == 0, np.sqrt(1.0 / GROUP), np.sqrt(2.0 / GROUP))
    basis = (scale * np.cos(np.pi * (2 * place + 1) * freq / (2 * GROUP))).astype(np.float32)
    rows = np.kron(np.eye(ROWS // GROUP, dtype=np.float32), basis)
    cols = np.kron(np.eye(WIDTH // GROUP, dtype=np.float32), basis).T
    spread = np.zeros((NX, WIDTH, 128), np.float32)
    for q in range(NX):
        spread[q, :, q * 32 : (q + 1) * 32] = cols
    return rows, spread


def split(value):
    high = value.astype(BF16)
    return high, (value - high.astype(F32)).astype(BF16)


def dot(a, b):
    return jnp.dot(a, b, preferred_element_type=F32)


def exact(a, b, dims):
    return lax.dot_general(a, b, (dims, ((), ())), precision=lax.Precision.HIGHEST, preferred_element_type=F32)


def kernel(
    grad_hbm, mom_hbm, rows_hbm, pair_hbm, spread_hbm, wide_hbm, mo_hbm, up_hbm,
    grad, mom, rows_t, pair_t, spread_t, wide_t, give, part, far_p, far_m, near_p, near_m, from_z,
    bands, bands_c, bands_z, bands_x, bands_y, bands_h, rest, mo, up,
    load_sem, out_sem, core_ss, core_rs, x_ss, x_rs, z_ss, z_rs, b_ss, b_rs, know,
):
    rep, f = lax.axis_index("rep"), lax.axis_index("fsdp")
    zh, y = rep // NY, rep % NY
    zl, x, c = f // (2 * NX), (f // 2) % NX, f % 2
    z = zh * NL + zl

    def device(dx=0, dy=0, dl=0, dz=0, dc=0):
        zz = (z + dz + NL * NH) % (NL * NH)
        low = (zz % NL + dl) % NL
        to_rep = (zz // NL) * NY + (y + dy + NY) % NY
        to_f = (low * NX + (x + dx + NX) % NX) * 2 + (c + dc) % 2
        return to_rep, to_f

    def signal(sem, **where):
        pl.semaphore_signal(sem, inc=1, device_id=device(**where), device_id_type=MESH)

    def send(src, dst, ss, rs, **where):
        copy = pltpu.make_async_remote_copy(
            src_ref=src, dst_ref=dst, send_sem=ss, recv_sem=rs, device_id=device(**where), device_id_type=MESH
        )
        copy.start()
        return copy

    barrier = pltpu.get_barrier_semaphore()
    near = (dict(dc=1), dict(dx=1), dict(dx=-1), dict(dy=1), dict(dy=-1), dict(dz=1), dict(dz=-1))
    for where in near:
        signal(barrier, **where)

    loads = [
        pltpu.make_async_copy(grad_hbm.at[0, 0, pl.ds(r0, n)], grad.at[pl.ds(r0, n)], load_sem.at[k])
        for k, (r0, n) in enumerate(PIECES)
    ]
    extra = [
        pltpu.make_async_copy(src, dst, load_sem.at[K + i])
        for i, (src, dst) in enumerate(
            ((rows_hbm, rows_t), (pair_hbm, pair_t), (spread_hbm, spread_t), (wide_hbm, wide_t), (mom_hbm.at[0], mom))
        )
    ]
    for copy in loads + extra:
        copy.start()

    def columns(slot, dl, core):
        owner = (((zl + dl) % NL) * NX + (x + STEP_OF_SLOT[slot]) % NX) * 2 + core
        return pl.ds(pl.multiple_of(owner * WIDTH, WIDTH), WIDTH)

    def convert(k):
        r0, n = PIECES[k]
        for slot in range(4):
            for dl in range(NL):
                give[slot, dl, pl.ds(r0, n)] = grad[pl.ds(r0, n), columns(slot, dl, 1 - c)].astype(F32)

    def add_own(k, slot):
        r0, n = PIECES[k]
        for dl in range(NL):
            part[slot, dl, pl.ds(r0, n)] += grad[pl.ds(r0, n), columns(slot, dl, c)].astype(F32)

    sent = []
    core_far, core_rest = {}, {}

    def give_piece(k):
        r0, n = PIECES[k]
        rows = pl.ds(r0, n)
        core_far[k] = send(
            give.at[pl.ds(FAR, 1), :, rows], part.at[pl.ds(FAR, 1), :, rows], core_ss.at[2 * k], core_rs.at[2 * k], dc=1
        )
        core_rest[k] = send(
            give.at[pl.ds(1, 3), :, rows], part.at[pl.ds(1, 3), :, rows], core_ss.at[2 * k + 1], core_rs.at[2 * k + 1], dc=1
        )
        sent.extend((core_far[k], core_rest[k]))

    loads[0].wait()
    convert(0)
    pl.semaphore_wait(barrier, len(near))
    give_piece(0)
    signal(know.at[0], dx=1)
    signal(know.at[1], dy=1)
    signal(know.at[2], dz=1)
    signal(know.at[3], dz=-1)
    for k in range(1, K):
        loads[k].wait()
        convert(k)
        give_piece(k)

    fars, nears, adds, zs = {}, {}, {}, {}

    def halves(k):
        r0, n = PIECES[k]
        return pl.ds(r0, n // 2), pl.ds(r0 + n // 2, n // 2), pl.ds(r0 // 2, n // 2)

    def open_piece(k):
        lower, upper, packed = halves(k)
        core_far[k].wait_recv()
        add_own(k, FAR)
        fars[k] = (
            send(part.at[FAR, :, lower], far_p.at[:, packed], x_ss.at[6 * k], x_rs.at[6 * k], dx=1),
            send(part.at[FAR, :, upper], far_m.at[:, packed], x_ss.at[6 * k + 1], x_rs.at[6 * k + 1], dx=-1),
        )
        core_rest[k].wait_recv()
        add_own(k, NEXT)
        add_own(k, PREV)
        nears[k] = (
            send(part.at[NEXT, :, upper], near_p.at[:, upper], x_ss.at[6 * k + 2], x_rs.at[6 * k + 2], dx=1),
            send(part.at[PREV, :, lower], near_m.at[:, lower], x_ss.at[6 * k + 3], x_rs.at[6 * k + 3], dx=-1),
        )
        add_own(k, OWN)
        sent.extend(fars[k] + nears[k])

    def pass_on(k):
        lower, upper, packed = halves(k)
        fars[k][0].wait_recv()
        part[NEXT, :, lower] += far_p[:, packed]
        first = send(part.at[NEXT, :, lower], near_p.at[:, lower], x_ss.at[6 * k + 4], x_rs.at[6 * k + 4], dx=1)
        fars[k][1].wait_recv()
        part[PREV, :, upper] += far_m[:, packed]
        second = send(part.at[PREV, :, upper], near_m.at[:, upper], x_ss.at[6 * k + 5], x_rs.at[6 * k + 5], dx=-1)
        adds[k] = (first, second)
        sent.extend(adds[k])

    def along_z(k):
        r0, n = PIECES[k]
        rows = pl.ds(r0, n)
        for copy in nears[k] + adds[k]:
            copy.wait_recv()
        zs[k] = []
        for dl in (3, 2, 1, 0):
            part[OWN, dl, rows] += near_p[dl, rows] + near_m[dl, rows]
            if dl:
                zs[k].append(
                    send(part.at[OWN, dl, rows], from_z.at[dl - 1, rows], z_ss.at[3 * k + dl - 1], z_rs.at[3 * k + dl - 1], dl=dl)
                )
        sent.extend(zs[k])

    outs = []

    def close(k):
        r0, n = PIECES[k]
        rows = pl.ds(r0, n)
        for copy in zs[k]:
            copy.wait_recv()
        mo[rows] = rest[rows] + ((part[OWN, 0, rows] + from_z[0, rows]) + (from_z[1, rows] + from_z[2, rows]))
        copy = pltpu.make_async_copy(mo.at[rows], mo_hbm.at[0, rows], out_sem.at[k])
        copy.start()
        outs.append(copy)

    def band_parts():
        for core in range(2):
            which = core
            owner_core = (c + core) % 2
            for dl in range(NL):
                total = jnp.zeros((2 * 16, 256), F32)
                for q in range(NX):
                    owner = (((zl + dl) % NL) * NX + q) * 2 + owner_core
                    block = grad[:, pl.ds(pl.multiple_of(owner * WIDTH, WIDTH), WIDTH)]
                    left = dot(pair_t[...], block)
                    high, low = split(left[:16] + left[16:])
                    total += dot(jnp.concatenate([high, low], axis=0), wide_t[q])
                bands[which, dl] = total[:16, :128] + total[:16, 128:] + total[16:, :128]

    def inverse(coeffs):
        return exact(rows_t[...], exact(coeffs, spread_t[x], ((1,), (1,))), ((0,), (0,)))

    def band_core():
        copy = send(bands.at[1], bands_c, b_ss.at[0], b_rs.at[0], dc=1)
        sent.append(copy)
        return copy

    def band_z(copy):
        copy.wait_recv()
        bands_c[...] += bands[0]
        copies = []
        for dl in (1, 2, 3):
            copies.append(send(bands_c.at[dl], bands_z.at[dl - 1], b_ss.at[dl], b_rs.at[dl], dl=dl))
        sent.extend(copies)
        return copies

    def band_x(copies):
        for copy in copies:
            copy.wait_recv()
        bands_x[0] = (bands_c[0] + bands_z[0]) + (bands_z[1] + bands_z[2])
        out = []
        for dx in (1, 2, 3):
            out.append(send(bands_x.at[0], bands_x.at[dx], b_ss.at[3 + dx], b_rs.at[3 + dx], dx=dx))
        sent.extend(out)
        return out

    def band_y(copies):
        for copy in copies:
            copy.wait_recv()
        total = (bands_x[0] + bands_x[1]) + (bands_x[2] + bands_x[3])
        own = exact(exact(rows_t[...], mom[...], ((1,), (0,))), spread_t[x], ((1,), (0,)))
        total = total + 0.999 * own
        bands_y[y] = total
        out = []
        for dy in (1, 2, 3):
            out.append(send(bands_y.at[y], bands_y.at[y], b_ss.at[6 + dy], b_rs.at[6 + dy], dy=dy))
        sent.extend(out)
        rest[...] = 0.999 * mom[...] - inverse(total)
        return out

    def band_h(copies):
        for copy in copies:
            copy.wait_recv()
        bands_h[zh] = (bands_y[0] + bands_y[1]) + (bands_y[2] + bands_y[3])
        out = []
        for dh in (1, 2, 3):
            out.append(send(bands_h.at[zh], bands_h.at[zh], b_ss.at[9 + dh], b_rs.at[9 + dh], dz=NL * dh))
        sent.extend(out)
        return out

    def band_end(copies):
        for copy in copies:
            copy.wait_recv()
        shared = ((bands_h[0] + bands_h[1]) + (bands_h[2] + bands_h[3])) * (1.0 / (NY * NH))
        up[...] = inverse(shared)
        copy = pltpu.make_async_copy(up, up_hbm, out_sem.at[K])
        copy.start()
        outs.append(copy)

    open_piece(0)
    for copy in extra:
        copy.wait()
    band_parts()
    b = band_core()
    pl.semaphore_wait(know.at[2], 1)
    pl.semaphore_wait(know.at[3], 1)
    signal(know.at[4], dz=1)
    signal(know.at[5], dz=-1)
    signal(know.at[6], dz=2)
    signal(know.at[7], dz=-2)
    open_piece(1)
    pass_on(0)
    pl.semaphore_wait(know.at[4], 1)
    pl.semaphore_wait(know.at[5], 1)
    b = band_z(b)
    open_piece(2)
    pass_on(1)
    pl.semaphore_wait(know.at[6], 1)
    pl.semaphore_wait(know.at[7], 1)
    signal(know.at[8], dz=4)
    along_z(0)
    pl.semaphore_wait(know.at[0], 1)
    b = band_x(b)
    open_piece(3)
    pass_on(2)
    along_z(1)
    pl.semaphore_wait(know.at[1], 1)
    b = band_y(b)
    pass_on(3)
    along_z(2)
    pl.semaphore_wait(know.at[8], 1)
    b = band_h(b)
    close(0)
    along_z(3)
    close(1)
    close(2)
    close(3)
    band_end(b)
    for copy in sent:
        copy.wait_send()
    for copy in outs:
        copy.wait()


def body(grad_parts, momentum):
    rows, spread = tables()
    rows_high = rows.astype(jnp.bfloat16)
    rows_low = (rows - rows_high.astype(np.float32)).astype(jnp.bfloat16)
    pair = np.concatenate([rows_high, rows_low], axis=0)
    spread_high = spread.astype(jnp.bfloat16)
    spread_low = (spread - spread_high.astype(np.float32)).astype(jnp.bfloat16)
    wide = np.concatenate([spread_high, spread_low], axis=2)
    any_space = pl.BlockSpec(memory_space=pl.ANY)
    vmem = pltpu.VMEM
    dma = pltpu.SemaphoreType.DMA
    out = pl.pallas_call(
        kernel,
        out_shape=(jax.ShapeDtypeStruct((1, ROWS, WIDTH), F32), jax.ShapeDtypeStruct((ROWS, WIDTH), F32)),
        in_specs=[any_space] * 6,
        out_specs=(any_space, any_space),
        scratch_shapes=[
            vmem((ROWS, 8192), BF16),
            vmem((ROWS, WIDTH), F32),
            vmem((16, ROWS), F32),
            vmem((32, ROWS), BF16),
            vmem((NX, WIDTH, 128), F32),
            vmem((NX, WIDTH, 256), BF16),
            vmem((4, NL, ROWS, WIDTH), F32),
            vmem((4, NL, ROWS, WIDTH), F32),
            vmem((NL, ROWS // 2, WIDTH), F32),
            vmem((NL, ROWS // 2, WIDTH), F32),
            vmem((NL, ROWS, WIDTH), F32),
            vmem((NL, ROWS, WIDTH), F32),
            vmem((3, ROWS, WIDTH), F32),
            vmem((2, NL, 16, 128), F32),
            vmem((NL, 16, 128), F32),
            vmem((3, 16, 128), F32),
            vmem((4, 16, 128), F32),
            vmem((4, 16, 128), F32),
            vmem((4, 16, 128), F32),
            vmem((ROWS, WIDTH), F32),
            vmem((ROWS, WIDTH), F32),
            vmem((ROWS, WIDTH), F32),
            dma((K + 5,)),
            dma((K + 1,)),
            dma((2 * K,)),
            dma((2 * K,)),
            dma((6 * K,)),
            dma((6 * K,)),
            dma((3 * K,)),
            dma((3 * K,)),
            dma((13,)),
            dma((13,)),
            pltpu.SemaphoreType.REGULAR((9,)),
        ],
        compiler_params=pltpu.CompilerParams(collective_id=0, has_side_effects=True, vmem_limit_bytes=60 * 2**20),
    )(
        grad_parts, momentum, jnp.asarray(rows), jnp.asarray(pair), jnp.asarray(spread), jnp.asarray(wide)
    )
    return out


def solution(mesh):
    in_specs = (P("rep", "fsdp", None, None), P("rep", None, "fsdp"))
    out_specs = (P("rep", None, "fsdp"), P(None, "fsdp"))
    return jax.shard_map(body, mesh=mesh, in_specs=in_specs, out_specs=out_specs, check_vma=False)
```

time: 231 us -> 50.2 us (0.22)
  the two profiles are of different devices: /device:TPU:128 before, /device:TPU:1 now
where the time goes in v1:
time: 50.2 us; the launch traced here: 50 us
  Pallas kernels  46.2 us (92%)
  local copies, waits for them, and re-layouts  3.14 us (6%)
  between operations  0.64 us (1%)
    pallas_call x1, Pallas kernels, body(): pl.pallas_call(kernel, out_shape=(jax.ShapeDtypeStruct((1, ROWS, WIDTH),...  46.2 us
    unnamed x2, local copies, waits for them, and re-layouts  3.14 us

profile of v1, /device:TPU:1, one launch (start us, length us, event | category | flops | bytes accessed | tf_op | source)
XLA Modules:
  0.0 50.0 jit_solution(6283716145755037511)
XLA Ops:
  0.6 46.2 %shard_map.77 = (f32[1,128,256]{2,1,0:T(8,128)}, f32[128,256]{1,0:T(8,128)}) custom-call(bf16[1,1,128,8192]{3,2,1,0:T(8,128)(2,1)} %grad_hbm.1, f32[1,128,256]{2,1,0:T(8,128)} %mom_hbm.1, f32[16,128]{1,0:T(8,128)} %constant.8.clone.rows_hbm, bf16[32,128]{1,0:T(8,128)(2,1)} %constant.9.clone.pair_hbm, f32[4,256,128]{2,1,0:T(8,128)} %constant.10.clone.spread_hbm, ...), custom_call_target="tpu_custom_call" | custom-call | tf_op jit(solution)/shard_map/pallas_call | solution.py:326
  46.9 1.6 %copy.10 = f32[1,128,256]{2,1,0:T(8,128)} copy(f32[1,128,256]{2,1,0:T(8,128)} %get-tuple-element.4) | data formatting | bytes 262144
  48.5 1.6 %copy.11 = f32[128,256]{1,0:T(8,128)} copy(f32[128,256]{1,0:T(8,128)} %get-tuple-element.5) | data formatting | bytes 262144

commit v2 on v1

v2 whole, which is shorter than its diff:
```python
import jax
import jax.numpy as jnp
import numpy as np
from jax import lax
from jax.experimental import pallas as pl
from jax.experimental.pallas import tpu as pltpu
from jax.sharding import PartitionSpec as P

MESH = pl.DeviceIdType.MESH
F32, BF16 = jnp.float32, jnp.bfloat16
GROUP, BAND = 64, 8
ROWS, WIDTH = 128, 256
NX = NY = NL = NH = 4

PIECES = ((0, 32), (32, 32), (64, 32), (96, 32))
K = len(PIECES)
FAR, NEXT, PREV, OWN = 0, 1, 2, 3
STEP_OF_SLOT = (2, 1, 3, 0)


def tables():
    freq = np.arange(BAND)[:, None]
    place = np.arange(GROUP)[None, :]
    scale = np.where(freq == 0, np.sqrt(1.0 / GROUP), np.sqrt(2.0 / GROUP))
    basis = (scale * np.cos(np.pi * (2 * place + 1) * freq / (2 * GROUP))).astype(np.float32)
    rows = np.kron(np.eye(ROWS // GROUP, dtype=np.float32), basis)
    cols = np.kron(np.eye(WIDTH // GROUP, dtype=np.float32), basis).T
    wide = np.zeros((2 * WIDTH, 128), np.float32)
    wide[:WIDTH, :32] = cols
    wide[WIDTH:, 32:64] = cols
    return basis, rows, wide


def split(value):
    high = value.astype(BF16)
    return high, (value - high.astype(F32)).astype(BF16)


def dot(a, b):
    return jnp.dot(a, b, preferred_element_type=F32)


def exact(a, b, dims):
    return lax.dot_general(a, b, (dims, ((), ())), precision=lax.Precision.HIGHEST, preferred_element_type=F32)


def kernel(
    grad_hbm, mom_hbm, basis_hbm, rows_hbm, wide_hbm, out, grad, mom, basis_t, rows_t, wide_t, give, part,
    far_p, far_m, near_p, near_m, from_z, left_t, bands, bands_c, bands_z, sums_z, bands_xy, sums_y, bands_h, rest,
    load_sem, core_ss, core_rs, x_ss, x_rs, z_ss, z_rs, b_ss, b_rs, know,
):
    rep, f = lax.axis_index("rep"), lax.axis_index("fsdp")
    zh, y = rep // NY, rep % NY
    zl, x, c = f // (2 * NX), (f // 2) % NX, f % 2
    z = zh * NL + zl

    def device(dx=0, dy=0, dl=0, dh=0, dc=0):
        to_rep = ((zh + dh) % NH) * NY + (y + dy) % NY
        to_f = (((zl + dl) % NL) * NX + (x + dx) % NX) * 2 + (c + dc) % 2
        return to_rep, to_f

    def signal(sem, **where):
        pl.semaphore_signal(sem, inc=1, device_id=device(**where), device_id_type=MESH)

    def prepare(src, dst, ss, rs, **where):
        return pltpu.make_async_remote_copy(
            src_ref=src, dst_ref=dst, send_sem=ss, recv_sem=rs, device_id=device(**where), device_id_type=MESH
        )

    def send(src, dst, ss, rs, **where):
        copy = prepare(src, dst, ss, rs, **where)
        copy.start()
        return copy

    barrier = pltpu.get_barrier_semaphore()
    signal(barrier, dc=1)
    for step in (1, 2, 3):
        signal(barrier, dx=step)
        signal(barrier, dy=step)
        signal(barrier, dl=step)

    @pl.when(zh == 0)
    def _():
        for step in (1, 2, 3):
            signal(barrier, dh=step)

    @pl.when((zh == 1) | (zh == 2))
    def _():
        signal(barrier, dh=1)

    @pl.when((zh == 2) | (zh == 3))
    def _():
        signal(barrier, dh=3)

    def pass_barrier():
        @pl.when(zh == 0)
        def _():
            pl.semaphore_wait(barrier, 10)

        @pl.when((zh == 1) | (zh == 3))
        def _():
            pl.semaphore_wait(barrier, 12)
            signal(know.at[0], dh=4 - zh)

        @pl.when(zh == 2)
        def _():
            pl.semaphore_wait(barrier, 13)
            signal(know.at[0], dh=2)
            signal(know.at[1], dh=1)
            signal(know.at[1], dh=3)

        for step in (1, 2, 3):
            signal(know.at[2], dx=step)

    loads = [
        pltpu.make_async_copy(grad_hbm.at[0, 0, pl.ds(r0, n)], grad.at[pl.ds(r0, n)], load_sem.at[k])
        for k, (r0, n) in enumerate(PIECES)
    ]
    extra = [
        pltpu.make_async_copy(src, dst, load_sem.at[K + i])
        for i, (src, dst) in enumerate(
            ((basis_hbm, basis_t), (rows_hbm, rows_t), (wide_hbm, wide_t), (mom_hbm.at[0], mom))
        )
    ]
    for copy in extra[:3] + loads + extra[3:]:
        copy.start()

    def columns(slot, dl, core):
        owner = (((zl + dl) % NL) * NX + (x + STEP_OF_SLOT[slot]) % NX) * 2 + core
        return pl.ds(pl.multiple_of(owner * WIDTH, WIDTH), WIDTH)

    def convert(k):
        r0, n = PIECES[k]
        for slot in range(4):
            for dl in range(NL):
                give[slot, dl, pl.ds(r0, n)] = grad[pl.ds(r0, n), columns(slot, dl, 1 - c)].astype(F32)

    def add_own(k, slot):
        r0, n = PIECES[k]
        for dl in range(NL):
            part[slot, dl, pl.ds(r0, n)] += grad[pl.ds(r0, n), columns(slot, dl, c)].astype(F32)

    sent = []
    core_far, core_rest = {}, {}

    def give_piece(k):
        r0, n = PIECES[k]
        rows = pl.ds(r0, n)
        core_far[k] = send(
            give.at[pl.ds(FAR, 1), :, rows], part.at[pl.ds(FAR, 1), :, rows], core_ss.at[2 * k], core_rs.at[2 * k], dc=1
        )
        core_rest[k] = send(
            give.at[pl.ds(1, 3), :, rows], part.at[pl.ds(1, 3), :, rows], core_ss.at[2 * k + 1], core_rs.at[2 * k + 1], dc=1
        )
        sent.extend((core_far[k], core_rest[k]))

    fars, nears, adds, zs = {}, {}, {}, {}

    def halves(k):
        r0, n = PIECES[k]
        return pl.ds(r0, n // 2), pl.ds(r0 + n // 2, n // 2), pl.ds(r0 // 2, n // 2)

    def open_piece(k):
        lower, upper, packed = halves(k)
        core_far[k].wait_recv()
        add_own(k, FAR)
        fars[k] = (
            send(part.at[FAR, :, lower], far_p.at[:, packed], x_ss.at[6 * k], x_rs.at[6 * k], dx=1),
            send(part.at[FAR, :, upper], far_m.at[:, packed], x_ss.at[6 * k + 1], x_rs.at[6 * k + 1], dx=-1),
        )
        core_rest[k].wait_recv()
        add_own(k, NEXT)
        add_own(k, PREV)
        nears[k] = (
            send(part.at[NEXT, :, upper], near_p.at[:, upper], x_ss.at[6 * k + 2], x_rs.at[6 * k + 2], dx=1),
            send(part.at[PREV, :, lower], near_m.at[:, lower], x_ss.at[6 * k + 3], x_rs.at[6 * k + 3], dx=-1),
        )
        add_own(k, OWN)
        sent.extend(fars[k] + nears[k])

    def pass_on(k):
        lower, upper, packed = halves(k)
        fars[k][0].wait_recv()
        part[NEXT, :, lower] += far_p[:, packed]
        first = send(part.at[NEXT, :, lower], near_p.at[:, lower], x_ss.at[6 * k + 4], x_rs.at[6 * k + 4], dx=1)
        fars[k][1].wait_recv()
        part[PREV, :, upper] += far_m[:, packed]
        second = send(part.at[PREV, :, upper], near_m.at[:, upper], x_ss.at[6 * k + 5], x_rs.at[6 * k + 5], dx=-1)
        adds[k] = (first, second)
        sent.extend(adds[k])

    def along_z(k):
        r0, n = PIECES[k]
        rows = pl.ds(r0, n)
        for copy in nears[k] + adds[k]:
            copy.wait_recv()
        zs[k] = []
        for dl in (3, 2, 1, 0):
            part[OWN, dl, rows] += near_p[dl, rows] + near_m[dl, rows]
            if dl:
                zs[k].append(
                    send(part.at[OWN, dl, rows], from_z.at[dl - 1, rows], z_ss.at[3 * k + dl - 1], z_rs.at[3 * k + dl - 1], dl=dl)
                )
        sent.extend(zs[k])

    def close(k):
        r0, n = PIECES[k]
        rows = pl.ds(r0, n)
        for copy in zs[k]:
            copy.wait_recv()
        out[0, rows] = rest[rows] + ((part[OWN, 0, rows] + from_z[0, rows]) + (from_z[1, rows] + from_z[2, rows]))

    def fold(left):
        high, low = split(jnp.concatenate([left[:8], left[8:]], axis=1))
        return jnp.concatenate([high, low], axis=0)

    def tile(both):
        return (both[:8, :128] + both[:8, 128:]) + both[8:, :128]

    def band_parts():
        step = 4
        for first in range(0, NL * NX * 2, step):
            left = dot(rows_t[...], grad[:, first * WIDTH : (first + step) * WIDTH])
            left = left[:16] + left[16:]
            for i in range(step):
                at = (first + i) * 16
                left_t[at : at + 16] = fold(left[:, i * WIDTH : (i + 1) * WIDTH])
        both = dot(left_t[...], wide_t[...])
        for owner in range(NL * NX * 2):
            which = (owner + c) % 2
            dl = (owner // (2 * NX) - zl + NL) % NL
            bands[which, dl, (owner // 2) % NX] = tile(both[owner * 16 : owner * 16 + 16])

    def band_of_momentum():
        high, low = split(mom[...])
        left = dot(rows_t[...], high)
        left = (left[:16] + left[16:]) + dot(rows_t[:16], low)
        return tile(dot(fold(left), wide_t[...]))

    def inverse(coeffs):
        high, low = split(coeffs)
        both = jnp.concatenate([high, low], axis=0)
        dims = (((1,), (1,)), ((), ()))
        one = lax.dot_general(both, wide_t[:, :128], dims, preferred_element_type=F32)
        two = lax.dot_general(both, wide_t[:, 128:], dims, preferred_element_type=F32)
        wide = (one[:8] + one[8:]) + two[:8]
        return [exact(basis_t[...], wide[:, i * WIDTH : (i + 1) * WIDTH], ((0,), (0,))) for i in range(2)]

    def band_core():
        copy = send(bands.at[1], bands_c, b_ss.at[0], b_rs.at[0], dc=1)
        sent.append(copy)
        return [copy]

    def band_z(copies):
        for copy in copies:
            copy.wait_recv()
        bands_c[...] += bands[0]
        copies = [send(bands_c.at[dl], bands_z.at[dl - 1], b_ss.at[dl], b_rs.at[dl], dl=dl) for dl in (2, 3, 1)]
        sent.extend(copies)
        return copies

    def band_xy(copies):
        for copy in copies:
            copy.wait_recv()
        sums_z[...] = (bands_c[0] + bands_z[0]) + (bands_z[1] + bands_z[2])
        sums_z[x] += 0.999 * band_of_momentum()
        bands_xy[y, 0] = sums_z[x]
        pl.semaphore_wait(know.at[2], 3)
        copies = []
        for dx in (2, 1, 3, 0):
            for dy in (2, 1, 3, 0):
                if dx or dy:
                    i = 4 + dx * 4 + dy
                    copies.append(send(sums_z.at[(x + dx) % NX], bands_xy.at[y, dx], b_ss.at[i], b_rs.at[i], dx=dx, dy=dy))
        sent.extend(copies)
        return copies

    def band_y(copies):
        for copy in copies:
            copy.wait_recv()
        for i in range(NY):
            sums_y[i] = (bands_xy[i, 0] + bands_xy[i, 1]) + (bands_xy[i, 2] + bands_xy[i, 3])
        bands_h[zh] = (sums_y[0] + sums_y[1]) + (sums_y[2] + sums_y[3])

    to_h = [None] + [prepare(bands_h.at[zh], bands_h.at[zh], b_ss.at[20 + dh], b_rs.at[20 + dh], dh=dh) for dh in (1, 2, 3)]

    def band_h():
        @pl.when(zh == 0)
        def _():
            pl.semaphore_wait(know.at[0], 3)

        to_h[1].start()
        to_h[3].start()

        @pl.when((zh == 1) | (zh == 3))
        def _():
            pl.semaphore_wait(know.at[1], 1)

        to_h[2].start()

    def find_rest():
        for i, value in enumerate(inverse(sums_y[y])):
            rows = pl.ds(i * GROUP, GROUP)
            rest[rows] = 0.999 * mom[rows] - value

    def band_end():
        for copy in to_h[1:]:
            copy.wait_recv()
        shared = ((bands_h[0] + bands_h[1]) + (bands_h[2] + bands_h[3])) * (1.0 / (NY * NH))
        for i, value in enumerate(inverse(shared)):
            out[1, pl.ds(i * GROUP, GROUP)] = value

    for copy in extra[:3] + loads:
        copy.wait()
    band_parts()
    convert(0)
    pass_barrier()
    b = band_core()
    give_piece(0)
    for k in range(1, K):
        convert(k)
        give_piece(k)
    extra[3].wait()
    b = band_z(b)
    open_piece(0)
    open_piece(1)
    pass_on(0)
    b = band_xy(b)
    open_piece(2)
    pass_on(1)
    open_piece(3)
    along_z(0)
    band_y(b)
    pl.when(zh > 0)(band_h)
    find_rest()
    pass_on(2)
    along_z(1)
    pass_on(3)
    along_z(2)
    close(0)
    pl.when(zh == 0)(band_h)
    along_z(3)
    close(1)
    close(2)
    close(3)
    band_end()
    for copy in sent + to_h[1:]:
        copy.wait_send()


def body(grad_parts, momentum):
    basis, rows, wide = tables()

    def halves(table, axis):
        high = table.astype(jnp.bfloat16)
        low = (table - high.astype(np.float32)).astype(jnp.bfloat16)
        return jnp.asarray(np.concatenate([high, low], axis=axis))

    operands = (grad_parts, momentum, jnp.asarray(basis), halves(rows, 0), halves(wide, 1))
    operands = [pltpu.with_memory_space_constraint(a, pltpu.HBM) for a in operands]
    vmem = pltpu.VMEM
    dma = pltpu.SemaphoreType.DMA
    tile = (8, 128)
    out = pl.pallas_call(
        kernel,
        out_shape=pltpu.VMEM((2, ROWS, WIDTH), F32),
        in_specs=[pl.BlockSpec(memory_space=pltpu.HBM)] * 5,
        out_specs=pl.BlockSpec(memory_space=pltpu.VMEM),
        scratch_shapes=[
            vmem((ROWS, 8192), BF16),
            vmem((ROWS, WIDTH), F32),
            vmem((BAND, GROUP), F32),
            vmem((32, ROWS), BF16),
            vmem((2 * WIDTH, 256), BF16),
            vmem((4, NL, ROWS, WIDTH), F32),
            vmem((4, NL, ROWS, WIDTH), F32),
            vmem((NL, ROWS // 2, WIDTH), F32),
            vmem((NL, ROWS // 2, WIDTH), F32),
            vmem((NL, ROWS, WIDTH), F32),
            vmem((NL, ROWS, WIDTH), F32),
            vmem((3, ROWS, WIDTH), F32),
            vmem((16 * NL * NX * 2, 2 * WIDTH), BF16),
            vmem((2, NL, NX, *tile), F32),
            vmem((NL, NX, *tile), F32),
            vmem((3, NX, *tile), F32),
            vmem((NX, *tile), F32),
            vmem((NY, NX, *tile), F32),
            vmem((NY, *tile), F32),
            vmem((NH, *tile), F32),
            vmem((ROWS, WIDTH), F32),
            dma((K + 4,)),
            dma((2 * K,)),
            dma((2 * K,)),
            dma((6 * K,)),
            dma((6 * K,)),
            dma((3 * K,)),
            dma((3 * K,)),
            dma((24,)),
            dma((24,)),
            pltpu.SemaphoreType.REGULAR((3,)),
        ],
        compiler_params=pltpu.CompilerParams(collective_id=0, has_side_effects=True, vmem_limit_bytes=56 * 2**20),
    )(*operands)
    return out[0][None], out[1]


def solution(mesh):
    in_specs = (P("rep", "fsdp", None, None), P("rep", None, "fsdp"))
    out_specs = (P("rep", None, "fsdp"), P(None, "fsdp"))
    return jax.shard_map(body, mesh=mesh, in_specs=in_specs, out_specs=out_specs, check_vma=False)
```

time: 50.2 us -> 41 us (0.82)
  the two profiles are of different devices: /device:TPU:1 before, /device:TPU:129 now
where the time goes in v2:
time: 41 us; the launch traced here: 40.8 us
  Pallas kernels  39.5 us (96%)
  local copies, waits for them, and re-layouts  0.72 us (2%)
  between operations  0.64 us (2%)
    pallas_call x1, Pallas kernels, body(): pl.pallas_call(kernel, out_shape=pltpu.VMEM((2, ROWS, WIDTH), F32), in_sp...  39.5 us

profile of v2, /device:TPU:129, one launch (start us, length us, event | category | flops | bytes accessed | tf_op | source)
XLA Modules:
  0.0 40.8 jit_solution(8419961600222755907)
XLA Ops:
  0.6 39.5 %shard_map.68 = f32[2,128,256]{2,1,0:T(8,128)S(1)} custom-call(bf16[1,1,128,8192]{3,2,1,0:T(8,128)(2,1)} %grad_hbm.1, f32[1,128,256]{2,1,0:T(8,128)} %mom_hbm.1, f32[8,64]{1,0:T(8,128)} %constant.6.clone.basis_hbm, bf16[32,128]{1,0:T(8,128)(2,1)} %constant.7.clone.rows_hbm, bf16[512,256]{1,0:T(8,128)(2,1)} %constant.8.clone.wide_hbm), custom_call_target="tpu_custom_call" | custom-call | tf_op jit(solution)/shard_map/pallas_call | solution.py:364
  40.1 0.7 %slice_bitcast_fusion = (f32[128,256]{1,0:T(8,128)}, f32[1,128,256]{2,1,0:T(8,128)}) fusion(f32[2,128,256]{2,1,0:T(8,128)S(1)} %shard_map.68), kind=kLoop, calls=%fused_computation | loop fusion | bytes 524288 | tf_op jit(solution)/shard_map/squeeze | solution.py:404

commit v3 on v2

--- a/solution.py
+++ b/solution.py
@@ -12,8 +12,10 @@
 ROWS, WIDTH = 128, 256
 NX = NY = NL = NH = 4
 
-PIECES = ((0, 32), (32, 32), (64, 32), (96, 32))
+PIECES = ((0, 16), (16, 32), (48, 32), (80, 32), (112, 16))
+Z_FIRST = (0,)
 K = len(PIECES)
+Z_ROWS = max(PIECES[k][0] + PIECES[k][1] for k in Z_FIRST)
 FAR, NEXT, PREV, OWN = 0, 1, 2, 3
 STEP_OF_SLOT = (2, 1, 3, 0)
 
@@ -46,7 +48,7 @@
 
 def kernel(
     grad_hbm, mom_hbm, basis_hbm, rows_hbm, wide_hbm, out, grad, mom, basis_t, rows_t, wide_t, give, part,
-    far_p, far_m, near_p, near_m, from_z, left_t, bands, bands_c, bands_z, sums_z, bands_xy, sums_y, bands_h, rest,
+    far_p, far_m, near_p, near_m, from_z, all_z, left_t, bands, bands_c, bands_z, sums_z, bands_xy, sums_y, bands_h, rest,
     load_sem, core_ss, core_rs, x_ss, x_rs, z_ss, z_rs, b_ss, b_rs, know,
 ):
     rep, f = lax.axis_index("rep"), lax.axis_index("fsdp")
@@ -55,7 +57,7 @@
     z = zh * NL + zl
 
     def device(dx=0, dy=0, dl=0, dh=0, dc=0):
-        to_rep = ((zh + dh) % NH) * NY + (y + dy) % NY
+        to_rep = ((zh + dh + NH) % NH) * NY + (y + dy) % NY
         to_f = (((zl + dl) % NL) * NX + (x + dx) % NX) * 2 + (c + dc) % 2
         return to_rep, to_f
 
@@ -79,35 +81,23 @@
         signal(barrier, dy=step)
         signal(barrier, dl=step)
 
-    @pl.when(zh == 0)
-    def _():
-        for step in (1, 2, 3):
+    for step in (1, 2, 3):
+
+        @pl.when(zh + step < NH)
+        def _(step=step):
             signal(barrier, dh=step)
 
-    @pl.when((zh == 1) | (zh == 2))
-    def _():
-        signal(barrier, dh=1)
-
-    @pl.when((zh == 2) | (zh == 3))
+    @pl.when(zh == 3)
     def _():
         signal(barrier, dh=3)
 
     def pass_barrier():
-        @pl.when(zh == 0)
-        def _():
-            pl.semaphore_wait(barrier, 10)
-
-        @pl.when((zh == 1) | (zh == 3))
-        def _():
-            pl.semaphore_wait(barrier, 12)
-            signal(know.at[0], dh=4 - zh)
-
-        @pl.when(zh == 2)
-        def _():
-            pl.semaphore_wait(barrier, 13)
-            signal(know.at[0], dh=2)
-            signal(know.at[1], dh=1)
-            signal(know.at[1], dh=3)
+        pl.semaphore_wait(barrier, 10 + zh + zh // 2 - zh // 3)
+        for step in (1, 2, 3):
+
+            @pl.when((zh >= step) & ((zh < 3) | (step > 1)))
+            def _(step=step):
+                signal(know.at[0], dh=-step)
 
         for step in (1, 2, 3):
             signal(know.at[2], dx=step)
@@ -160,32 +150,46 @@
         r0, n = PIECES[k]
         return pl.ds(r0, n // 2), pl.ds(r0 + n // 2, n // 2), pl.ds(r0 // 2, n // 2)
 
+    def members(k):
+        return pl.ds(0, 1 if k in Z_FIRST else NL)
+
+    def send_far(k):
+        lower, upper, packed = halves(k)
+        dls = members(k)
+        fars[k] = (
+            send(part.at[FAR, dls, lower], far_p.at[dls, packed], x_ss.at[6 * k], x_rs.at[6 * k], dx=1),
+            send(part.at[FAR, dls, upper], far_m.at[dls, packed], x_ss.at[6 * k + 1], x_rs.at[6 * k + 1], dx=-1),
+        )
+        sent.extend(fars[k])
+
+    def send_near(k):
+        lower, upper, packed = halves(k)
+        dls = members(k)
+        nears[k] = (
+            send(part.at[NEXT, dls, upper], near_p.at[dls, upper], x_ss.at[6 * k + 2], x_rs.at[6 * k + 2], dx=1),
+            send(part.at[PREV, dls, lower], near_m.at[dls, lower], x_ss.at[6 * k + 3], x_rs.at[6 * k + 3], dx=-1),
+        )
+        sent.extend(nears[k])
+
     def open_piece(k):
-        lower, upper, packed = halves(k)
         core_far[k].wait_recv()
         add_own(k, FAR)
-        fars[k] = (
-            send(part.at[FAR, :, lower], far_p.at[:, packed], x_ss.at[6 * k], x_rs.at[6 * k], dx=1),
-            send(part.at[FAR, :, upper], far_m.at[:, packed], x_ss.at[6 * k + 1], x_rs.at[6 * k + 1], dx=-1),
-        )
+        send_far(k)
         core_rest[k].wait_recv()
         add_own(k, NEXT)
         add_own(k, PREV)
-        nears[k] = (
-            send(part.at[NEXT, :, upper], near_p.at[:, upper], x_ss.at[6 * k + 2], x_rs.at[6 * k + 2], dx=1),
-            send(part.at[PREV, :, lower], near_m.at[:, lower], x_ss.at[6 * k + 3], x_rs.at[6 * k + 3], dx=-1),
-        )
+        send_near(k)
         add_own(k, OWN)
-        sent.extend(fars[k] + nears[k])
 
     def pass_on(k):
         lower, upper, packed = halves(k)
+        dls = members(k)
         fars[k][0].wait_recv()
-        part[NEXT, :, lower] += far_p[:, packed]
-        first = send(part.at[NEXT, :, lower], near_p.at[:, lower], x_ss.at[6 * k + 4], x_rs.at[6 * k + 4], dx=1)
+        part[NEXT, dls, lower] += far_p[dls, packed]
+        first = send(part.at[NEXT, dls, lower], near_p.at[dls, lower], x_ss.at[6 * k + 4], x_rs.at[6 * k + 4], dx=1)
         fars[k][1].wait_recv()
-        part[PREV, :, upper] += far_m[:, packed]
-        second = send(part.at[PREV, :, upper], near_m.at[:, upper], x_ss.at[6 * k + 5], x_rs.at[6 * k + 5], dx=-1)
+        part[PREV, dls, upper] += far_m[dls, packed]
+        second = send(part.at[PREV, dls, upper], near_m.at[dls, upper], x_ss.at[6 * k + 5], x_rs.at[6 * k + 5], dx=-1)
         adds[k] = (first, second)
         sent.extend(adds[k])
 
@@ -209,6 +213,37 @@
         for copy in zs[k]:
             copy.wait_recv()
         out[0, rows] = rest[rows] + ((part[OWN, 0, rows] + from_z[0, rows]) + (from_z[1, rows] + from_z[2, rows]))
+
+    def z_first(k):
+        r0, n = PIECES[k]
+        rows = pl.ds(r0, n)
+        core_far[k].wait_recv()
+        core_rest[k].wait_recv()
+        for slot in range(4):
+            add_own(k, slot)
+        zs[k] = [
+            send(part.at[:, dl, rows], all_z.at[dl - 1, :, rows], z_ss.at[3 * k + dl - 1], z_rs.at[3 * k + dl - 1], dl=dl)
+            for dl in (3, 2, 1)
+        ]
+        sent.extend(zs[k])
+
+    def x_second(k):
+        r0, n = PIECES[k]
+        rows = pl.ds(r0, n)
+        for copy in zs[k]:
+            copy.wait_recv()
+        for slot in range(4):
+            part[slot, 0, rows] += (all_z[0, slot, rows] + all_z[1, slot, rows]) + all_z[2, slot, rows]
+            if slot == FAR:
+                send_far(k)
+        send_near(k)
+
+    def close_x(k):
+        r0, n = PIECES[k]
+        rows = pl.ds(r0, n)
+        for copy in nears[k] + adds[k]:
+            copy.wait_recv()
+        out[0, rows] = rest[rows] + (part[OWN, 0, rows] + (near_p[0, rows] + near_m[0, rows]))
 
     def fold(left):
         high, low = split(jnp.concatenate([left[:8], left[8:]], axis=1))
@@ -289,14 +324,17 @@
         def _():
             pl.semaphore_wait(know.at[0], 3)
 
-        to_h[1].start()
-        to_h[3].start()
-
-        @pl.when((zh == 1) | (zh == 3))
+        @pl.when(zh != 1)
         def _():
-            pl.semaphore_wait(know.at[1], 1)
-
-        to_h[2].start()
+            for dh in (2, 1, 3):
+                to_h[dh].start()
+
+        @pl.when(zh == 1)
+        def _():
+            to_h[3].start()
+            pl.semaphore_wait(know.at[0], 2)
+            to_h[2].start()
+            to_h[1].start()
 
     def find_rest():
         for i, value in enumerate(inverse(sums_y[y])):
@@ -313,36 +351,45 @@
     for copy in extra[:3] + loads:
         copy.wait()
     band_parts()
-    convert(0)
+    convert(1)
     pass_barrier()
     b = band_core()
+    give_piece(1)
+    convert(0)
     give_piece(0)
-    for k in range(1, K):
-        convert(k)
-        give_piece(k)
+    convert(2)
+    give_piece(2)
     extra[3].wait()
     b = band_z(b)
-    open_piece(0)
     open_piece(1)
-    pass_on(0)
+    z_first(0)
+    convert(3)
+    give_piece(3)
+    open_piece(2)
+    convert(4)
+    give_piece(4)
+    pass_on(1)
     b = band_xy(b)
-    open_piece(2)
-    pass_on(1)
     open_piece(3)
-    along_z(0)
+    pass_on(2)
+    x_second(0)
+    open_piece(4)
+    along_z(1)
     band_y(b)
     pl.when(zh > 0)(band_h)
     find_rest()
-    pass_on(2)
-    along_z(1)
     pass_on(3)
+    pass_on(0)
     along_z(2)
-    close(0)
+    pass_on(4)
+    along_z(3)
+    close_x(0)
+    close(1)
     pl.when(zh == 0)(band_h)
-    along_z(3)
-    close(1)
     close(2)
+    along_z(4)
     close(3)
+    close(4)
     band_end()
     for copy in sent + to_h[1:]:
         copy.wait_send()
@@ -379,6 +426,7 @@
             vmem((NL, ROWS, WIDTH), F32),
             vmem((NL, ROWS, WIDTH), F32),
             vmem((3, ROWS, WIDTH), F32),
+            vmem((3, 4, Z_ROWS, WIDTH), F32),
             vmem((16 * NL * NX * 2, 2 * WIDTH), BF16),
             vmem((2, NL, NX, *tile), F32),
             vmem((NL, NX, *tile), F32),

time: 41 us -> 38.4 us (0.937)
  the two profiles are of different devices: /device:TPU:129 before, /device:TPU:1 now
where the time goes in v3:
time: 38.4 us; the launch traced here: 38.3 us
  Pallas kernels  36.9 us (96%)
  local copies, waits for them, and re-layouts  0.72 us (2%)
  between operations  0.64 us (2%)
    pallas_call x1, Pallas kernels, body(): pl.pallas_call(kernel, out_shape=pltpu.VMEM((2, ROWS, WIDTH), F32), in_sp...  36.9 us

profile of v3, /device:TPU:1, one launch (start us, length us, event | category | flops | bytes accessed | tf_op | source)
XLA Modules:
  0.0 38.3 jit_solution(12332940178212872824)
XLA Ops:
  0.6 36.9 %shard_map.68 = f32[2,128,256]{2,1,0:T(8,128)S(1)} custom-call(bf16[1,1,128,8192]{3,2,1,0:T(8,128)(2,1)} %grad_hbm.1, f32[1,128,256]{2,1,0:T(8,128)} %mom_hbm.1, f32[8,64]{1,0:T(8,128)} %constant.6.clone.basis_hbm, bf16[32,128]{1,0:T(8,128)(2,1)} %constant.7.clone.rows_hbm, bf16[512,256]{1,0:T(8,128)(2,1)} %constant.8.clone.wide_hbm), custom_call_target="tpu_custom_call" | custom-call | tf_op jit(solution)/shard_map/pallas_call | solution.py:411
  37.6 0.7 %slice_bitcast_fusion = (f32[128,256]{1,0:T(8,128)}, f32[1,128,256]{2,1,0:T(8,128)}) fusion(f32[2,128,256]{2,1,0:T(8,128)S(1)} %shard_map.68), kind=kLoop, calls=%fused_computation | loop fusion | bytes 524288 | tf_op jit(solution)/shard_map/squeeze | solution.py:452

commit v4 on v3

--- a/solution.py
+++ b/solution.py
@@ -52,14 +52,17 @@
     load_sem, core_ss, core_rs, x_ss, x_rs, z_ss, z_rs, b_ss, b_rs, know,
 ):
     rep, f = lax.axis_index("rep"), lax.axis_index("fsdp")
-    zh, y = rep // NY, rep % NY
-    zl, x, c = f // (2 * NX), (f // 2) % NX, f % 2
-    z = zh * NL + zl
+    zh, y = lax.div(rep, NY), lax.rem(rep, NY)
+    zl, x, c = lax.div(f, 2 * NX), lax.rem(lax.div(f, 2), NX), lax.rem(f, 2)
+
+    x_on = [2 * lax.rem(x + i, NX) for i in range(NX)]
+    l_on = [2 * NX * lax.rem(zl + i, NL) for i in range(NL)]
+    y_on = [lax.rem(y + i, NY) for i in range(NY)]
+    h_on = [NY * lax.rem(zh + i, NH) for i in range(NH)]
+    c_on = [c, 1 - c]
 
     def device(dx=0, dy=0, dl=0, dh=0, dc=0):
-        to_rep = ((zh + dh + NH) % NH) * NY + (y + dy) % NY
-        to_f = (((zl + dl) % NL) * NX + (x + dx) % NX) * 2 + (c + dc) % 2
-        return to_rep, to_f
+        return h_on[dh % NH] + y_on[dy % NY], l_on[dl % NL] + x_on[dx % NX] + c_on[dc]
 
     def signal(sem, **where):
         pl.semaphore_signal(sem, inc=1, device_id=device(**where), device_id_type=MESH)
@@ -75,11 +78,13 @@
         return copy
 
     barrier = pltpu.get_barrier_semaphore()
+    for step in (3, 2, 1):
+        signal(barrier, dl=step)
+    for step in (2, 1, 3):
+        signal(barrier, dx=step)
+    for step in (2, 1, 3):
+        signal(barrier, dy=step)
     signal(barrier, dc=1)
-    for step in (1, 2, 3):
-        signal(barrier, dx=step)
-        signal(barrier, dy=step)
-        signal(barrier, dl=step)
 
     for step in (1, 2, 3):
 
@@ -92,7 +97,7 @@
         signal(barrier, dh=3)
 
     def pass_barrier():
-        pl.semaphore_wait(barrier, 10 + zh + zh // 2 - zh // 3)
+        pl.semaphore_wait(barrier, 10 + zh + lax.div(zh, 2) - lax.div(zh, 3))
         for step in (1, 2, 3):
 
             @pl.when((zh >= step) & ((zh < 3) | (step > 1)))
@@ -116,21 +121,26 @@
         copy.start()
 
     def columns(slot, dl, core):
-        owner = (((zl + dl) % NL) * NX + (x + STEP_OF_SLOT[slot]) % NX) * 2 + core
+        owner = l_on[dl] + x_on[STEP_OF_SLOT[slot]] + c_on[core]
         return pl.ds(pl.multiple_of(owner * WIDTH, WIDTH), WIDTH)
 
     def convert(k):
         r0, n = PIECES[k]
         for slot in range(4):
             for dl in range(NL):
-                give[slot, dl, pl.ds(r0, n)] = grad[pl.ds(r0, n), columns(slot, dl, 1 - c)].astype(F32)
+                give[slot, dl, pl.ds(r0, n)] = grad[pl.ds(r0, n), columns(slot, dl, 1)].astype(F32)
 
     def add_own(k, slot):
         r0, n = PIECES[k]
         for dl in range(NL):
-            part[slot, dl, pl.ds(r0, n)] += grad[pl.ds(r0, n), columns(slot, dl, c)].astype(F32)
+            part[slot, dl, pl.ds(r0, n)] += grad[pl.ds(r0, n), columns(slot, dl, 0)].astype(F32)
 
     sent = []
+
+    def drain():
+        while sent:
+            sent.pop(0).wait_send()
+
     core_far, core_rest = {}, {}
 
     def give_piece(k):
@@ -262,9 +272,9 @@
                 left_t[at : at + 16] = fold(left[:, i * WIDTH : (i + 1) * WIDTH])
         both = dot(left_t[...], wide_t[...])
         for owner in range(NL * NX * 2):
-            which = (owner + c) % 2
-            dl = (owner // (2 * NX) - zl + NL) % NL
-            bands[which, dl, (owner // 2) % NX] = tile(both[owner * 16 : owner * 16 + 16])
+            which = c_on[owner % 2]
+            dl = lax.rem(owner // (2 * NX) - zl + NL, NL)
+            bands[which, dl, owner // 2 % NX] = tile(both[owner * 16 : owner * 16 + 16])
 
     def band_of_momentum():
         high, low = split(mom[...])
@@ -306,7 +316,7 @@
             for dy in (2, 1, 3, 0):
                 if dx or dy:
                     i = 4 + dx * 4 + dy
-                    copies.append(send(sums_z.at[(x + dx) % NX], bands_xy.at[y, dx], b_ss.at[i], b_rs.at[i], dx=dx, dy=dy))
+                    copies.append(send(sums_z.at[lax.div(x_on[dx], 2)], bands_xy.at[y, dx], b_ss.at[i], b_rs.at[i], dx=dx, dy=dy))
         sent.extend(copies)
         return copies
 
@@ -319,22 +329,12 @@
 
     to_h = [None] + [prepare(bands_h.at[zh], bands_h.at[zh], b_ss.at[20 + dh], b_rs.at[20 + dh], dh=dh) for dh in (1, 2, 3)]
 
-    def band_h():
-        @pl.when(zh == 0)
-        def _():
-            pl.semaphore_wait(know.at[0], 3)
-
-        @pl.when(zh != 1)
-        def _():
-            for dh in (2, 1, 3):
-                to_h[dh].start()
-
-        @pl.when(zh == 1)
-        def _():
-            to_h[3].start()
-            pl.semaphore_wait(know.at[0], 2)
-            to_h[2].start()
-            to_h[1].start()
+    def band_h(first):
+        if first < 2:
+            to_h[3].start() if first == 1 else None
+            pl.semaphore_wait(know.at[0], 3 - first)
+        for dh in (2, 1) if first == 1 else (2, 1, 3):
+            to_h[dh].start()
 
     def find_rest():
         for i, value in enumerate(inverse(sums_y[y])):
@@ -348,51 +348,152 @@
         for i, value in enumerate(inverse(shared)):
             out[1, pl.ds(i * GROUP, GROUP)] = value
 
-    for copy in extra[:3] + loads:
-        copy.wait()
-    band_parts()
-    convert(1)
-    pass_barrier()
-    b = band_core()
-    give_piece(1)
-    convert(0)
-    give_piece(0)
-    convert(2)
-    give_piece(2)
-    extra[3].wait()
-    b = band_z(b)
-    open_piece(1)
-    z_first(0)
-    convert(3)
-    give_piece(3)
-    open_piece(2)
-    convert(4)
-    give_piece(4)
-    pass_on(1)
-    b = band_xy(b)
-    open_piece(3)
-    pass_on(2)
-    x_second(0)
-    open_piece(4)
-    along_z(1)
-    band_y(b)
-    pl.when(zh > 0)(band_h)
-    find_rest()
-    pass_on(3)
-    pass_on(0)
-    along_z(2)
-    pass_on(4)
-    along_z(3)
-    close_x(0)
-    close(1)
-    pl.when(zh == 0)(band_h)
-    close(2)
-    along_z(4)
-    close(3)
-    close(4)
-    band_end()
-    for copy in sent + to_h[1:]:
-        copy.wait_send()
+    @pl.when(zh == 0)
+    def _():
+        for copy in extra[:3] + loads:
+            copy.wait()
+        convert(1)
+        pass_barrier()
+        give_piece(1)
+        convert(2)
+        give_piece(2)
+        convert(0)
+        give_piece(0)
+        convert(3)
+        give_piece(3)
+        convert(4)
+        give_piece(4)
+        band_parts()
+        b = band_core()
+        extra[3].wait()
+        open_piece(1)
+        b = band_z(b)
+        z_first(0)
+        open_piece(2)
+        pass_on(1)
+        b = band_xy(b)
+        open_piece(3)
+        pass_on(2)
+        open_piece(4)
+        along_z(1)
+        pass_on(3)
+        x_second(0)
+        along_z(2)
+        band_y(b)
+        find_rest()
+        pass_on(4)
+        pass_on(0)
+        along_z(3)
+        close(1)
+        band_h(0)
+        close(2)
+        drain()
+        along_z(4)
+        close_x(0)
+        close(3)
+        band_end()
+        close(4)
+        drain()
+        for copy in to_h[1:]:
+            copy.wait_send()
+
+    @pl.when(zh == 1)
+    def _():
+        for copy in extra[:3] + loads:
+            copy.wait()
+        band_parts()
+        convert(1)
+        pass_barrier()
+        b = band_core()
+        give_piece(1)
+        convert(2)
+        give_piece(2)
+        extra[3].wait()
+        b = band_z(b)
+        open_piece(1)
+        convert(0)
+        give_piece(0)
+        convert(3)
+        give_piece(3)
+        convert(4)
+        give_piece(4)
+        z_first(0)
+        b = band_xy(b)
+        open_piece(2)
+        pass_on(1)
+        open_piece(3)
+        band_y(b)
+        band_h(1)
+        pass_on(2)
+        find_rest()
+        open_piece(4)
+        along_z(1)
+        pass_on(3)
+        x_second(0)
+        along_z(2)
+        pass_on(4)
+        pass_on(0)
+        along_z(3)
+        close(1)
+        close(2)
+        drain()
+        along_z(4)
+        close_x(0)
+        close(3)
+        band_end()
+        close(4)
+        drain()
+        for copy in to_h[1:]:
+            copy.wait_send()
+
+    @pl.when(zh >= 2)
+    def _():
+        for copy in extra[:3] + loads:
+            copy.wait()
+        band_parts()
+        convert(1)
+        pass_barrier()
+        b = band_core()
+        give_piece(1)
+        convert(2)
+        give_piece(2)
+        extra[3].wait()
+        b = band_z(b)
+        open_piece(1)
+        convert(0)
+        give_piece(0)
+        convert(3)
+        give_piece(3)
+        convert(4)
+        give_piece(4)
+        z_first(0)
+        b = band_xy(b)
+        open_piece(2)
+        pass_on(1)
+        open_piece(3)
+        band_y(b)
+        band_h(2)
+        pass_on(2)
+        find_rest()
+        open_piece(4)
+        along_z(1)
+        pass_on(3)
+        x_second(0)
+        along_z(2)
+        pass_on(4)
+        pass_on(0)
+        along_z(3)
+        close(1)
+        close(2)
+        drain()
+        along_z(4)
+        close_x(0)
+        close(3)
+        band_end()
+        close(4)
+        drain()
+        for copy in to_h[1:]:
+            copy.wait_send()
 
 
 def body(grad_parts, momentum):

time: 38.4 us -> 36.9 us (0.961)
  Pallas kernels: 36.9 us -> 35.2 us
    pallas_call x1, Pallas kernels: 36.9 us -> 35.2 us  [body(): pl.pallas_call(kernel, out_shape=pltpu.VMEM((2, ROWS, WIDTH), F32), in_sp...]
where the time goes in v4:
time: 36.9 us; the launch traced here: 36.5 us
  Pallas kernels  35.2 us (95%)
  local copies, waits for them, and re-layouts  0.72 us (2%)
  between operations  0.64 us (2%)
    pallas_call x1, Pallas kernels, body(): pl.pallas_call(kernel, out_shape=pltpu.VMEM((2, ROWS, WIDTH), F32), in_sp...  35.2 us

profile of v4, /device:TPU:1, one launch (start us, length us, event | category | flops | bytes accessed | tf_op | source)
XLA Modules:
  0.0 36.5 jit_solution(16912956874803829871)
XLA Ops:
  0.6 35.2 %shard_map.68 = f32[2,128,256]{2,1,0:T(8,128)S(1)} custom-call(bf16[1,1,128,8192]{3,2,1,0:T(8,128)(2,1)} %grad_hbm.1, f32[1,128,256]{2,1,0:T(8,128)} %mom_hbm.1, f32[8,64]{1,0:T(8,128)} %constant.6.clone.basis_hbm, bf16[32,128]{1,0:T(8,128)(2,1)} %constant.7.clone.rows_hbm, bf16[512,256]{1,0:T(8,128)(2,1)} %constant.8.clone.wide_hbm), custom_call_target="tpu_custom_call" | custom-call | tf_op jit(solution)/shard_map/pallas_call | solution.py:512
  35.8 0.7 %slice_bitcast_fusion = (f32[128,256]{1,0:T(8,128)}, f32[1,128,256]{2,1,0:T(8,128)}) fusion(f32[2,128,256]{2,1,0:T(8,128)S(1)} %shard_map.68), kind=kLoop, calls=%fused_computation | loop fusion | bytes 524288 | tf_op jit(solution)/shard_map/squeeze | solution.py:553

commit v5 on v4

--- a/solution.py
+++ b/solution.py
@@ -78,34 +78,112 @@
         return copy
 
     barrier = pltpu.get_barrier_semaphore()
-    for step in (3, 2, 1):
-        signal(barrier, dl=step)
-    for step in (2, 1, 3):
-        signal(barrier, dx=step)
-    for step in (2, 1, 3):
-        signal(barrier, dy=step)
+    inner = (zl == 1) | (zl == 2)
+    late = zh >= 2
+    edge = ((zh == 2) & (zl == 3)) | ((zh == 3) & (zl == 0))
+
+    @pl.when(late)
+    def _():
+        for step in (3, 2, 1):
+            signal(barrier, dl=step)
+        for step in (2, 1, 3):
+            signal(barrier, dx=step)
+        for step in (2, 1, 3):
+            signal(barrier, dy=step)
+
+    @pl.when(jnp.logical_not(late))
+    def _():
+        for step in (1, 3):
+            signal(barrier, dx=step)
+            signal(barrier, dy=step)
+
+        @pl.when(zl < 3)
+        def _():
+            signal(barrier, dl=1)
+
+        @pl.when(zl > 0)
+        def _():
+            signal(barrier, dl=3)
+
     signal(barrier, dc=1)
 
-    for step in (1, 2, 3):
-
-        @pl.when(zh + step < NH)
-        def _(step=step):
+    @pl.when(zh == 0)
+    def _():
+        for step in (1, 2, 3):
             signal(barrier, dh=step)
 
-    @pl.when(zh == 3)
+    @pl.when(zh == 1)
     def _():
-        signal(barrier, dh=3)
-
-    def pass_barrier():
-        pl.semaphore_wait(barrier, 10 + zh + lax.div(zh, 2) - lax.div(zh, 3))
+        for step in (1, 2):
+            signal(barrier, dh=step)
+
+    def meet(sem):
+        @pl.when((zh == 2) & (zl == 3))
+        def _():
+            signal(sem, dh=1, dl=1)
+
+        @pl.when((zh == 3) & (zl == 0))
+        def _():
+            signal(sem, dh=3, dl=3)
+
+    meet(barrier)
+
+    def pass_barrier(early):
+        if early:
+            pl.semaphore_wait(barrier, 6 + lax.rem(lax.div(zl + 1, 2), 2) + zh)
+            signal(know.at[3], dx=1)
+            signal(know.at[4], dy=1)
+
+            @pl.when(inner)
+            def _():
+                signal(know.at[5], dl=1)
+                signal(know.at[5], dl=3)
+
+        else:
+            pl.semaphore_wait(barrier, 12 + jnp.where(edge, 1, 0))
+            meet(know.at[3])
+            tell_y()
         for step in (1, 2, 3):
 
             @pl.when((zh >= step) & ((zh < 3) | (step > 1)))
             def _(step=step):
                 signal(know.at[0], dh=-step)
 
+    def tell_y():
         for step in (1, 2, 3):
             signal(know.at[2], dx=step)
+
+    def learn_xy():
+        pl.semaphore_wait(know.at[3], 1)
+        pl.semaphore_wait(know.at[4], 1)
+        tell_y()
+
+    def learn_z():
+        pl.semaphore_wait(know.at[5], 1)
+
+        @pl.when(zl == 1)
+        def _():
+            signal(know.at[6], dl=3)
+
+        @pl.when(zl == 2)
+        def _():
+            signal(know.at[6], dl=1)
+
+        @pl.when(jnp.logical_not(inner))
+        def _():
+            pl.semaphore_wait(know.at[6], 1)
+
+    def pass_meeting():
+        @pl.when(edge)
+        def _():
+            pl.semaphore_wait(know.at[3], 1)
+            for step in (1, 2, 3):
+                signal(know.at[4], dl=step)
+
+    def learn_meeting():
+        @pl.when(jnp.logical_not(edge))
+        def _():
+            pl.semaphore_wait(know.at[4], 1)
 
     loads = [
         pltpu.make_async_copy(grad_hbm.at[0, 0, pl.ds(r0, n)], grad.at[pl.ds(r0, n)], load_sem.at[k])
@@ -117,7 +195,7 @@
             ((basis_hbm, basis_t), (rows_hbm, rows_t), (wide_hbm, wide_t), (mom_hbm.at[0], mom))
         )
     ]
-    for copy in extra[:3] + loads + extra[3:]:
+    for copy in [loads[1]] + extra[:3] + [loads[2], loads[0]] + loads[3:] + extra[3:]:
         copy.start()
 
     def columns(slot, dl, core):
@@ -330,9 +408,12 @@
     to_h = [None] + [prepare(bands_h.at[zh], bands_h.at[zh], b_ss.at[20 + dh], b_rs.at[20 + dh], dh=dh) for dh in (1, 2, 3)]
 
     def band_h(first):
+        if first == 1:
+            to_h[3].start()
         if first < 2:
-            to_h[3].start() if first == 1 else None
             pl.semaphore_wait(know.at[0], 3 - first)
+        else:
+            learn_meeting()
         for dh in (2, 1) if first == 1 else (2, 1, 3):
             to_h[dh].start()
 
@@ -350,11 +431,12 @@
 
     @pl.when(zh == 0)
     def _():
-        for copy in extra[:3] + loads:
+        loads[1].wait()
+        convert(1)
+        pass_barrier(True)
+        give_piece(1)
+        for copy in extra[:3] + loads[:1] + loads[2:]:
             copy.wait()
-        convert(1)
-        pass_barrier()
-        give_piece(1)
         convert(2)
         give_piece(2)
         convert(0)
@@ -363,27 +445,29 @@
         give_piece(3)
         convert(4)
         give_piece(4)
+        open_piece(1)
+        learn_xy()
+        open_piece(2)
+        learn_z()
+        z_first(0)
         band_parts()
         b = band_core()
+        pass_on(1)
         extra[3].wait()
-        open_piece(1)
         b = band_z(b)
-        z_first(0)
-        open_piece(2)
-        pass_on(1)
-        b = band_xy(b)
         open_piece(3)
         pass_on(2)
         open_piece(4)
         along_z(1)
         pass_on(3)
+        b = band_xy(b)
         x_second(0)
         along_z(2)
-        band_y(b)
-        find_rest()
         pass_on(4)
         pass_on(0)
         along_z(3)
+        band_y(b)
+        find_rest()
         close(1)
         band_h(0)
         close(2)
@@ -399,27 +483,30 @@
 
     @pl.when(zh == 1)
     def _():
-        for copy in extra[:3] + loads:
+        loads[1].wait()
+        convert(1)
+        pass_barrier(True)
+        give_piece(1)
+        for copy in extra[:3] + loads[:1] + loads[2:]:
             copy.wait()
-        band_parts()
-        convert(1)
-        pass_barrier()
-        b = band_core()
-        give_piece(1)
         convert(2)
         give_piece(2)
+        band_parts()
+        b = band_core()
         extra[3].wait()
-        b = band_z(b)
         open_piece(1)
+        learn_xy()
         convert(0)
         give_piece(0)
         convert(3)
         give_piece(3)
         convert(4)
         give_piece(4)
+        open_piece(2)
+        learn_z()
+        b = band_z(b)
         z_first(0)
         b = band_xy(b)
-        open_piece(2)
         pass_on(1)
         open_piece(3)
         band_y(b)
@@ -448,11 +535,12 @@
 
     @pl.when(zh >= 2)
     def _():
-        for copy in extra[:3] + loads:
+        loads[1].wait()
+        for copy in extra[:3] + loads[:1] + loads[2:]:
             copy.wait()
         band_parts()
         convert(1)
-        pass_barrier()
+        pass_barrier(False)
         b = band_core()
         give_piece(1)
         convert(2)
@@ -460,6 +548,7 @@
         extra[3].wait()
         b = band_z(b)
         open_piece(1)
+        pass_meeting()
         convert(0)
         give_piece(0)
         convert(3)
@@ -546,7 +635,7 @@
             dma((3 * K,)),
             dma((24,)),
             dma((24,)),
-            pltpu.SemaphoreType.REGULAR((3,)),
+            pltpu.SemaphoreType.REGULAR((7,)),
         ],
         compiler_params=pltpu.CompilerParams(collective_id=0, has_side_effects=True, vmem_limit_bytes=56 * 2**20),
     )(*operands)

time: 36.9 us -> 36.6 us (level)
  no operation moved by 1% of the time
where the time goes in v5:
time: 36.6 us; the launch traced here: 36.5 us
  Pallas kernels  35.1 us (96%)
  local copies, waits for them, and re-layouts  0.72 us (2%)
  between operations  0.64 us (2%)
    pallas_call x1, Pallas kernels, body(): pl.pallas_call(kernel, out_shape=pltpu.VMEM((2, ROWS, WIDTH), F32), in_sp...  35.1 us

profile of v5, /device:TPU:1, one launch (start us, length us, event | category | flops | bytes accessed | tf_op | source)
XLA Modules:
  0.0 36.5 jit_solution(4445141429684869984)
XLA Ops:
  0.6 35.1 %shard_map.68 = f32[2,128,256]{2,1,0:T(8,128)S(1)} custom-call(bf16[1,1,128,8192]{3,2,1,0:T(8,128)(2,1)} %grad_hbm.1, f32[1,128,256]{2,1,0:T(8,128)} %mom_hbm.1, f32[8,64]{1,0:T(8,128)} %constant.6.clone.basis_hbm, bf16[32,128]{1,0:T(8,128)(2,1)} %constant.7.clone.rows_hbm, bf16[512,256]{1,0:T(8,128)(2,1)} %constant.8.clone.wide_hbm), custom_call_target="tpu_custom_call" | custom-call | tf_op jit(solution)/shard_map/pallas_call | solution.py:601
  35.7 0.7 %slice_bitcast_fusion = (f32[128,256]{1,0:T(8,128)}, f32[1,128,256]{2,1,0:T(8,128)}) fusion(f32[2,128,256]{2,1,0:T(8,128)S(1)} %shard_map.68), kind=kLoop, calls=%fused_computation | loop fusion | bytes 524288 | tf_op jit(solution)/shard_map/squeeze | solution.py:642

commit v6 on v5

--- a/solution.py
+++ b/solution.py
@@ -441,22 +441,22 @@
         give_piece(2)
         convert(0)
         give_piece(0)
+        open_piece(1)
+        learn_xy()
         convert(3)
         give_piece(3)
         convert(4)
         give_piece(4)
-        open_piece(1)
-        learn_xy()
         open_piece(2)
         learn_z()
         z_first(0)
+        pass_on(1)
+        open_piece(3)
         band_parts()
         b = band_core()
-        pass_on(1)
+        pass_on(2)
         extra[3].wait()
         b = band_z(b)
-        open_piece(3)
-        pass_on(2)
         open_piece(4)
         along_z(1)
         pass_on(3)

time: 36.6 us -> 36.6 us (level)
  no operation moved by 1% of the time
where the time goes in v6:
time: 36.6 us; the launch traced here: 36.5 us
  Pallas kernels  35.1 us (96%)
  local copies, waits for them, and re-layouts  0.72 us (2%)
  between operations  0.64 us (2%)
    pallas_call x1, Pallas kernels, body(): pl.pallas_call(kernel, out_shape=pltpu.VMEM((2, ROWS, WIDTH), F32), in_sp...  35.1 us

profile of v6, /device:TPU:1, one launch (start us, length us, event | category | flops | bytes accessed | tf_op | source)
XLA Modules:
  0.0 36.5 jit_solution(12008206030200564044)
XLA Ops:
  0.6 35.1 %shard_map.68 = f32[2,128,256]{2,1,0:T(8,128)S(1)} custom-call(bf16[1,1,128,8192]{3,2,1,0:T(8,128)(2,1)} %grad_hbm.1, f32[1,128,256]{2,1,0:T(8,128)} %mom_hbm.1, f32[8,64]{1,0:T(8,128)} %constant.6.clone.basis_hbm, bf16[32,128]{1,0:T(8,128)(2,1)} %constant.7.clone.rows_hbm, bf16[512,256]{1,0:T(8,128)(2,1)} %constant.8.clone.wide_hbm), custom_call_target="tpu_custom_call" | custom-call | tf_op jit(solution)/shard_map/pallas_call | solution.py:601
  35.7 0.7 %slice_bitcast_fusion = (f32[128,256]{1,0:T(8,128)}, f32[1,128,256]{2,1,0:T(8,128)}) fusion(f32[2,128,256]{2,1,0:T(8,128)S(1)} %shard_map.68), kind=kLoop, calls=%fused_computation | loop fusion | bytes 524288 | tf_op jit(solution)/shard_map/squeeze | solution.py:642
